TPU v7x, 128 devices: a whole 4x4x4 slice. The times are simulated.
128 devices in a mesh: group: 8 (over y_hi, x), row: 16 (over z, y_lo, core).
Axes of the slice: x: 4, y: 4 (y_hi: 2, y_lo: 2; y = y_hi * 2 + y_lo), z: 4, core: 2. Of those that a mesh axis runs over, the one named last changes fastest.
Arguments:
- embeds: bfloat16 [65536, 768], P(('group', 'row')), may hold values from -120 to 120
- member: int32 [65536], P(('group', 'row')), may hold values from 0 to 7, as said below
Outputs:
- nearest: float32 [65536], P(('group', 'row'))
Inputs may be any that keep to these rules, and one draw needn't show every extreme that they name: `member`: rows come in aligned blocks of 512; no cluster takes more than 128 rows of one block. For each remainder of the block index modulo the row axis's size, one cluster takes exactly 128 rows of every block with that remainder.
All inputs are finite; a program needn't handle non-finite values.
Results may differ from a plain program's by a relative error of at most 0.00056.
Values may be sent and summed in bfloat16 or wider, within the bound.
No kernel may reach another device: no remote copies, remote signals or barrier semaphores. Data moves between devices by JAX's collectives and lax.ppermute only.
A program may use at most 128 MiB of HBM per device.

v0:
```python
import math
import jax
import jax.numpy as jnp
from jax import lax
from jax.sharding import PartitionSpec as P

absent = -4.0


def block_maxima(own_rows, own_flags, column_rows, column_flags, own_ids, column_ids):
    stride = math.gcd(column_rows.shape[0], 2048)
    number = column_rows.shape[0] // stride
    pieces = column_rows.reshape(number, stride, column_rows.shape[1])
    piece_flags = column_flags.reshape(number, stride)
    piece_ids = column_ids.reshape(number, stride)
    own_keep = own_flags > 0

    def visit(row_best, item):
        piece_rows, flags_part, ids_part = item
        scores = lax.dot_general(
            own_rows, piece_rows, (((1,), (1,)), ((), ())), preferred_element_type=jnp.float32
        )
        keep = (
            own_keep[:, None] & (flags_part[None, :] > 0) & (own_ids[:, None] != ids_part[None, :])
        )
        masked = jnp.where(keep, scores, absent)
        return (jnp.maximum(row_best, jnp.max(masked, axis=1)), jnp.max(masked, axis=0))

    start_best = jnp.full((own_rows.shape[0],), absent, jnp.float32)
    row_best, column_best = lax.scan(visit, start_best, (pieces, piece_flags, piece_ids))
    return (row_best, column_best.reshape(-1))


def on_device(embeds, member):
    groups = lax.axis_size("group")
    block_rows = embeds.shape[0]
    per_cluster = 2 * block_rows // groups
    capacity = groups * per_cluster
    values = embeds.astype(jnp.float32)
    normed = (values * lax.rsqrt(jnp.sum(values * values, axis=1, keepdims=True) + 1e-06)).astype(
        jnp.bfloat16
    )
    hits = (member[:, None] == jnp.arange(groups, dtype=jnp.int32)[None, :]).astype(jnp.int32)
    ranking = jnp.sum(jnp.cumsum(hits, axis=0) * hits, axis=1) - 1
    target = member * per_cluster + ranking
    placer = (jnp.arange(capacity, dtype=jnp.int32)[:, None] == target[None, :]).astype(
        jnp.bfloat16
    )
    outgoing = jnp.dot(placer, normed, preferred_element_type=jnp.float32).astype(jnp.bfloat16)
    counts = jnp.sum(hits, axis=0)
    filled = (jnp.arange(per_cluster, dtype=jnp.int32)[None, :] < counts[:, None]).astype(
        jnp.bfloat16
    )
    arrived, arrived_flags = (
        lax.all_to_all(
            outgoing.reshape(groups, per_cluster, -1),
            "group",
            split_axis=0,
            concat_axis=0,
            tiled=True,
        ),
        lax.all_to_all(filled, "group", split_axis=0, concat_axis=0, tiled=True),
    )
    own_rows = arrived.reshape(capacity, -1)
    own_flags = arrived_flags.reshape(capacity)
    own_ids = lax.axis_index("row") * capacity + jnp.arange(capacity, dtype=jnp.int32)
    initial = jnp.full((capacity,), absent, jnp.float32)
    column_rows = lax.all_gather(own_rows, "row", axis=0, tiled=True)
    column_flags = lax.all_gather(own_flags, "row", axis=0, tiled=True)
    column_ids = jnp.arange(column_rows.shape[0], dtype=jnp.int32)
    found, unused_columns = block_maxima(
        own_rows, own_flags, column_rows, column_flags, own_ids, column_ids
    )
    nearest = jnp.maximum(initial, found)
    homeward = lax.all_to_all(
        nearest.reshape(groups, per_cluster), "group", split_axis=0, concat_axis=0, tiled=True
    )
    return homeward.reshape(-1)[target]


def solution(mesh):
    in_specs = (P(("group", "row"), None), P(("group", "row")))
    out_specs = P(("group", "row"))
    return jax.shard_map(
        on_device, mesh=mesh, in_specs=in_specs, out_specs=out_specs, check_vma=False
    )
```

profile of v0, /device:TPU:0, one launch (start us, length us, event | category | flops | bytes accessed | tf_op | source)
XLA Modules:
  0.0 246.7 jit_solution(17565139092833224877)
XLA Ops:
  6.5 0.0 all-gather.2.cloned.1.call-start
  6.5 0.7 fusion.14
  7.2 1.1 reduce-window.6
  8.4 0.2 slice_reduce_fusion
  8.6 0.9 fusion.13
  9.5 0.7 compare_select_fusion
  10.2 1.4 fusion.8
  11.5 2.3 fusion.7
  13.8 29.7 %all_to_all.20 = bf16[8,128,768]{2,1,0:T(8,128)(2,1)} all-to-all(bf16[8,128,768]{2,1,0:T(8,128)(2,1)S(1)} %bitcast.34), channel_id=1, replica_groups=mesh['group'=8,'row'=16] {'group'}, dimensions={0} | all-to-all | bytes 3145728 | tf_op jit(solution)/shard_map/all_to_all | solution.py:55
  43.6 0.0 all-gather.2.cloned.1.call-update
  43.6 0.7 compare_convert_fusion
  44.3 3.3 %all-to-all-start = ((bf16[8,1,128]{2,1,0:T(2,128)(2,1)}), bf16[8,1,128]{2,1,0:T(2,128)(2,1)S(1)}, u32[]{:S(2)}, u32[]{:S(2)}) async-start(bf16[8,1,128]{2,1,0:T(2,128)(2,1)} %compare_convert_fusion), calls=%async_computation | async-start | bytes 8192 | tf_op jit(solution)/shard_map/all_to_all | solution.py:62
  47.6 7.6 %all-to-all-done = bf16[8,1,128]{2,1,0:T(2,128)(2,1)S(1)} async-done(((bf16[8,1,128]{2,1,0:T(2,128)(2,1)}), bf16[8,1,128]{2,1,0:T(2,128)(2,1)S(1)}, u32[]{:S(2)}, u32[]{:S(2)}) %all-to-all-start) | async-done | bytes 2080 | tf_op jit(solution)/shard_map/all_to_all | solution.py:62
  55.2 20.3 %all_gather.6 = bf16[16384]{0:T(1024)(128)(2,1)S(1)} all-gather(bf16[1024]{0:T(1024)(128)(2,1)S(1)} %bitcast.37), channel_id=1, replica_groups=mesh['group'=8,'row'=16] {'row'}, dimensions={0}, use_global_device_ids=true | all-gather | bytes 34816 | tf_op jit(solution)/shard_map/all_gather | solution.py:69
  75.5 97.8 %all-gather.2.cloned.1.call-done = bf16[16384,768]{1,0:T(8,128)(2,1)} async-done(((bf16[1024,768]{1,0:T(8,128)(2,1)}), bf16[16384,768]{1,0:T(8,128)(2,1)}) %all-gather.2.cloned.1.call-update) | async-done | bytes 25165840 | tf_op jit(solution)/shard_map/all_gather | solution.py:68
  173.3 48.2 %while.11 = (s32[]{:T(128)}, f32[1024]{0:T(1024)S(1)}, pred[1024]{0:T(1024)(128)(4,1)S(1)}, bf16[8,2048]{1,0:T(8,128)(2,1)S(1)}, s32[8,2048]{1,0:T(8,128)S(1)}, ...) while((s32[]{:T(128)}, f32[1024]{0:T(1024)S(1)}, ...), condition=%wide.region_7.8_spmd.clone, body=%wide.region_5.7_spmd.clone.sunk | while | flops 3231719424 | bytes 4777595 | solution.py:30
  173.4 5.9 %fusion.21 = f32[1024]{0:T(1024)S(1)} fusion(bf16[1024,768]{1,0:T(8,128)(2,1)} %get-tuple-element.173, s32[1024]{0:T(1024)S(1)} %iota_add_fusion.2, s32[2048]{0:T(1024)S(1)} %bitcast.35, pred[1024]{0:T(1024)(128)(4,1)S(1)} %get-tuple-element.169, pred[2048]{0:T(1024)(128)(4,1)S(1)} %compare_reduce_fusion.2, ...), kind=kOutput, calls=%fused_computation.3.clone.1 | convolution fusion | flops 3231710208 | bytes 4738560 | tf_op jit(solution)/shard_map/while/body/eval_jaxpr/dot_general | solution.py:20
  179.4 5.9 %fusion.21 = f32[1024]{0:T(1024)S(1)} fusion(bf16[1024,768]{1,0:T(8,128)(2,1)} %get-tuple-element.173, s32[1024]{0:T(1024)S(1)} %iota_add_fusion.2, s32[2048]{0:T(1024)S(1)} %bitcast.35, pred[1024]{0:T(1024)(128)(4,1)S(1)} %get-tuple-element.169, pred[2048]{0:T(1024)(128)(4,1)S(1)} %compare_reduce_fusion.2, ...), kind=kOutput, calls=%fused_computation.3.clone.1 | convolution fusion | flops 3231710208 | bytes 4738560 | tf_op jit(solution)/shard_map/while/body/eval_jaxpr/dot_general | solution.py:20
  185.4 5.9 %fusion.21 = f32[1024]{0:T(1024)S(1)} fusion(bf16[1024,768]{1,0:T(8,128)(2,1)} %get-tuple-element.173, s32[1024]{0:T(1024)S(1)} %iota_add_fusion.2, s32[2048]{0:T(1024)S(1)} %bitcast.35, pred[1024]{0:T(1024)(128)(4,1)S(1)} %get-tuple-element.169, pred[2048]{0:T(1024)(128)(4,1)S(1)} %compare_reduce_fusion.2, ...), kind=kOutput, calls=%fused_computation.3.clone.1 | convolution fusion | flops 3231710208 | bytes 4738560 | tf_op jit(solution)/shard_map/while/body/eval_jaxpr/dot_general | solution.py:20
  191.5 5.9 %fusion.21 = f32[1024]{0:T(1024)S(1)} fusion(bf16[1024,768]{1,0:T(8,128)(2,1)} %get-tuple-element.173, s32[1024]{0:T(1024)S(1)} %iota_add_fusion.2, s32[2048]{0:T(1024)S(1)} %bitcast.35, pred[1024]{0:T(1024)(128)(4,1)S(1)} %get-tuple-element.169, pred[2048]{0:T(1024)(128)(4,1)S(1)} %compare_reduce_fusion.2, ...), kind=kOutput, calls=%fused_computation.3.clone.1 | convolution fusion | flops 3231710208 | bytes 4738560 | tf_op jit(solution)/shard_map/while/body/eval_jaxpr/dot_general | solution.py:20
  197.5 5.9 %fusion.21 = f32[1024]{0:T(1024)S(1)} fusion(bf16[1024,768]{1,0:T(8,128)(2,1)} %get-tuple-element.173, s32[1024]{0:T(1024)S(1)} %iota_add_fusion.2, s32[2048]{0:T(1024)S(1)} %bitcast.35, pred[1024]{0:T(1024)(128)(4,1)S(1)} %get-tuple-element.169, pred[2048]{0:T(1024)(128)(4,1)S(1)} %compare_reduce_fusion.2, ...), kind=kOutput, calls=%fused_computation.3.clone.1 | convolution fusion | flops 3231710208 | bytes 4738560 | tf_op jit(solution)/shard_map/while/body/eval_jaxpr/dot_general | solution.py:20
  203.5 5.9 %fusion.21 = f32[1024]{0:T(1024)S(1)} fusion(bf16[1024,768]{1,0:T(8,128)(2,1)} %get-tuple-element.173, s32[1024]{0:T(1024)S(1)} %iota_add_fusion.2, s32[2048]{0:T(1024)S(1)} %bitcast.35, pred[1024]{0:T(1024)(128)(4,1)S(1)} %get-tuple-element.169, pred[2048]{0:T(1024)(128)(4,1)S(1)} %compare_reduce_fusion.2, ...), kind=kOutput, calls=%fused_computation.3.clone.1 | convolution fusion | flops 3231710208 | bytes 4738560 | tf_op jit(solution)/shard_map/while/body/eval_jaxpr/dot_general | solution.py:20
  209.6 5.9 %fusion.21 = f32[1024]{0:T(1024)S(1)} fusion(bf16[1024,768]{1,0:T(8,128)(2,1)} %get-tuple-element.173, s32[1024]{0:T(1024)S(1)} %iota_add_fusion.2, s32[2048]{0:T(1024)S(1)} %bitcast.35, pred[1024]{0:T(1024)(128)(4,1)S(1)} %get-tuple-element.169, pred[2048]{0:T(1024)(128)(4,1)S(1)} %compare_reduce_fusion.2, ...), kind=kOutput, calls=%fused_computation.3.clone.1 | convolution fusion | flops 3231710208 | bytes 4738560 | tf_op jit(solution)/shard_map/while/body/eval_jaxpr/dot_general | solution.py:20
  215.6 5.9 %fusion.21 = f32[1024]{0:T(1024)S(1)} fusion(bf16[1024,768]{1,0:T(8,128)(2,1)} %get-tuple-element.173, s32[1024]{0:T(1024)S(1)} %iota_add_fusion.2, s32[2048]{0:T(1024)S(1)} %bitcast.35, pred[1024]{0:T(1024)(128)(4,1)S(1)} %get-tuple-element.169, pred[2048]{0:T(1024)(128)(4,1)S(1)} %compare_reduce_fusion.2, ...), kind=kOutput, calls=%fused_computation.3.clone.1 | convolution fusion | flops 3231710208 | bytes 4738560 | tf_op jit(solution)/shard_map/while/body/eval_jaxpr/dot_general | solution.py:20
  221.5 0.6 broadcast_maximum_fusion
  222.1 6.7 %all-to-all-start.2 = ((f32[8,1,128]{2,1,0:T(1,128)}), f32[8,1,128]{2,1,0:T(1,128)S(1)}, u32[]{:S(2)}, u32[]{:S(2)}) async-start(f32[8,1,128]{2,1,0:T(1,128)} %bitcast.6), calls=%async_computation.2 | async-start | bytes 8192 | tf_op jit(solution)/shard_map/all_to_all | solution.py:75
  228.8 7.7 %all-to-all-done.2 = f32[8,1,128]{2,1,0:T(1,128)S(1)} async-done(((f32[8,1,128]{2,1,0:T(1,128)}), f32[8,1,128]{2,1,0:T(1,128)S(1)}, u32[]{:S(2)}, u32[]{:S(2)}) %all-to-all-start.2) | async-done | bytes 4128 | tf_op jit(solution)/shard_map/all_to_all | solution.py:75
  236.5 3.4 %gather_fusion = f32[512]{0:T(512)} fusion(f32[1024]{0:T(1024)S(1)} %bitcast.31, s32[1024]{0:T(1024)S(1)} %pad_clamp_fusion), kind=kCustom, calls=%fused_computation | custom fusion | bytes 6144 | tf_op jit(solution)/shard_map/gather | solution.py:78
  (41 shorter events, 0.7 us)
Async XLA Ops:
  6.5 166.8 %all-gather.2.cloned.1.call-start = ((), (), s32[]{:S(2)}) async-start(), calls=%async_computation.3 | async-start | bytes 26738688 | tf_op jit(solution)/shard_map/all_gather | solution.py:68
  44.3 10.9 %all-to-all-start = ((bf16[8,1,128]{2,1,0:T(2,128)(2,1)}), bf16[8,1,128]{2,1,0:T(2,128)(2,1)S(1)}, u32[]{:S(2)}, u32[]{:S(2)}) async-start(bf16[8,1,128]{2,1,0:T(2,128)(2,1)} %compare_convert_fusion), calls=%async_computation | async-start | bytes 8192 | tf_op jit(solution)/shard_map/all_to_all | solution.py:62
  222.1 14.4 %all-to-all-start.2 = ((f32[8,1,128]{2,1,0:T(1,128)}), f32[8,1,128]{2,1,0:T(1,128)S(1)}, u32[]{:S(2)}, u32[]{:S(2)}) async-start(f32[8,1,128]{2,1,0:T(1,128)} %bitcast.6), calls=%async_computation.2 | async-start | bytes 8192 | tf_op jit(solution)/shard_map/all_to_all | solution.py:75
Sparse Core Ops, SparseCore 0:
  43.7 129.5 all-gather.1
where the time goes:
time: 247 us
  waiting for transfers between devices  113 us (46%)
  blocking collectives  50.1 us (20%)
  matrix products  49.6 us (20%)
  between operations  13.5 us (5%)
  starting transfers between devices  9.97 us (4%)
  other arithmetic  6.56 us (3%)
  local copies, waits for them, and re-layouts  3.74 us (2%)
    all_gather x1, waiting for transfers between devices, on_device(): column_rows = lax.all_gather(own_rows, 'row', axis=0, tiled=True)  97.8 us
    dot_general x8, matrix products, visit(): lax.dot_general(own_rows, piece_rows, (((1,), (1,)), ((), ())), preferred...  47.3 us
    all_to_all x1, blocking collectives, on_device(): lax.all_to_all(outgoing.reshape(groups, per_cluster, -1), 'group', split_...  29.7 us
    all_gather x1, blocking collectives, on_device(): column_flags = lax.all_gather(own_flags, 'row', axis=0, tiled=True)  20.3 us
    all_to_all x1, waiting for transfers between devices, on_device(): lax.all_to_all(nearest.reshape(groups, per_cluster), 'group', split_axis=...  7.65 us
    all_to_all x1, waiting for transfers between devices, on_device(): lax.all_to_all(filled, 'group', split_axis=0, concat_axis=0, tiled=True)  7.56 us
    all_to_all x1, starting transfers between devices, on_device(): lax.all_to_all(nearest.reshape(groups, per_cluster), 'group', split_axis=...  6.71 us
  transfers between devices with their start and end apart: 3, of which 3 were waited for; matrix products, arithmetic and copies ran while one was open for 0% of the time, Pallas kernels for 0%

commit v1 on v0

--- a/solution.py
+++ b/solution.py
@@ -65,7 +65,9 @@
     own_flags = arrived_flags.reshape(capacity)
     own_ids = lax.axis_index("row") * capacity + jnp.arange(capacity, dtype=jnp.int32)
     initial = jnp.full((capacity,), absent, jnp.float32)
-    column_rows = lax.all_gather(own_rows, "row", axis=0, tiled=True)
+    column_rows = jnp.concatenate(
+        lax.all_to_all(jnp.stack([own_rows] * lax.axis_size("row")), "row", 0, 0), axis=0
+    )
     column_flags = lax.all_gather(own_flags, "row", axis=0, tiled=True)
     column_ids = jnp.arange(column_rows.shape[0], dtype=jnp.int32)
     found, unused_columns = block_maxima(

time: 247 us -> 405 us (1.64)
  blocking collectives: 50.1 us -> 312 us
  waiting for transfers between devices: 113 us -> 11 us
  between operations: 13.5 us -> 0.08 us
  local copies, waits for them, and re-layouts: 3.74 us -> 12.3 us
  starting transfers between devices: 9.97 us -> 15.9 us
    all_gather x1, blocking collectives: 20.3 us -> 286 us  [on_device(): column_flags = lax.all_gather(own_flags, 'row', axis=0, tiled=True)]
    all_gather x1 -> x0, waiting for transfers between devices: 97.8 us -> none  [on_device(): column_rows = lax.all_gather(own_rows, 'row', axis=0, tiled=True)]
    another operation x1 -> x2, local copies, waits for them, and re-layouts: 0.01 us -> 8.59 us  [the longest x1 8.58 us: on_device(): jnp.stack([own_rows] * lax.axis_size('row'))]
    all_to_all x0 -> x1, starting transfers between devices: none -> 5.57 us  [on_device(): lax.all_to_all(jnp.stack([own_rows] * lax.axis_size('row')), 'row', 0, 0)]
    all_to_all x1, waiting for transfers between devices: 7.56 us -> 3.3 us  [on_device(): lax.all_to_all(filled, 'group', split_axis=0, concat_axis=0, tiled=True)]
  transfers between devices with their start and end apart: 3 -> 3, of which waited for: 3 -> 2; matrix products, arithmetic and copies ran while one was open for 0% -> 1% of each run, Pallas kernels for 0% -> 0%
where the time goes in v1:
time: 405 us; the launch traced here: 404 us
  blocking collectives  312 us (77%)
  matrix products  45.8 us (11%)
  starting transfers between devices  15.9 us (4%)
  local copies, waits for them, and re-layouts  12.3 us (3%)
  waiting for transfers between devices  11 us (3%)
  other arithmetic  6.57 us (2%)
    all_gather x1, blocking collectives, on_device(): column_flags = lax.all_gather(own_flags, 'row', axis=0, tiled=True)  286 us
    dot_general x8, matrix products, visit(): lax.dot_general(own_rows, piece_rows, (((1,), (1,)), ((), ())), preferred...  43.5 us
    all_to_all x1, blocking collectives, on_device(): lax.all_to_all(outgoing.reshape(groups, per_cluster, -1), 'group', split_...  26 us
    another operation x1, local copies, waits for them, and re-layouts, on_device(): jnp.stack([own_rows] * lax.axis_size('row'))  8.58 us
  transfers between devices with their start and end apart: 3, of which 2 were waited for; matrix products, arithmetic and copies ran while one was open for 1% of the time, Pallas kernels for 0%

profile of v1, /device:TPU:0, one launch (start us, length us, event | category | flops | bytes accessed | tf_op | source)
XLA Modules:
  0.0 404.3 jit_solution(17635833564164960105)
XLA Ops:
  0.0 0.7 fusion.14
  0.7 1.1 reduce-window.6
  1.8 0.2 slice_reduce_fusion
  2.1 0.9 fusion.13
  3.0 0.7 compare_convert_fusion
  3.6 7.0 %all-to-all-start = ((bf16[8,1,128]{2,1,0:T(2,128)(2,1)}), bf16[8,1,128]{2,1,0:T(2,128)(2,1)S(1)}, u32[]{:S(2)}, u32[]{:S(2)}) async-start(bf16[8,1,128]{2,1,0:T(2,128)(2,1)} %compare_convert_fusion), calls=%async_computation | async-start | bytes 8192 | tf_op jit(solution)/shard_map/all_to_all | solution.py:62
  10.6 0.7 compare_select_fusion
  11.3 1.4 fusion.8
  12.7 2.3 fusion.7
  15.0 3.3 all-to-all-done
  18.3 26.0 %all_to_all.25 = bf16[8,128,768]{2,1,0:T(8,128)(2,1)S(1)} all-to-all(bf16[8,128,768]{2,1,0:T(8,128)(2,1)S(1)} %bitcast.34), channel_id=1, replica_groups=mesh['group'=8,'row'=16] {'group'}, dimensions={0} | all-to-all | bytes 3145728 | tf_op jit(solution)/shard_map/all_to_all | solution.py:55
  44.3 8.6 %stack.3 = bf16[16,1024,768]{2,1,0:T(8,128)(2,1)} broadcast(bf16[1024,768]{1,0:T(8,128)(2,1)S(1)} %bitcast.32), dimensions={1,2} | broadcast | bytes 26738688 | tf_op jit(solution)/shard_map/stack | solution.py:69
  52.9 5.6 %all-to-all-start.2 = ((bf16[16,1024,768]{2,1,0:T(8,128)(2,1)}), bf16[16,1024,768]{2,1,0:T(8,128)(2,1)}, u32[]{:S(2)}, u32[]{:S(2)}) async-start(bf16[16,1024,768]{2,1,0:T(8,128)(2,1)} %stack.3), calls=%async_computation.2 | async-start | bytes 50331648 | tf_op jit(solution)/shard_map/all_to_all | solution.py:69
  58.5 286.3 %all_gather.3 = bf16[16384]{0:T(1024)(128)(2,1)S(1)} all-gather(bf16[1024]{0:T(1024)(128)(2,1)S(1)} %bitcast.37), channel_id=1, replica_groups=mesh['group'=8,'row'=16] {'row'}, dimensions={0}, use_global_device_ids=true | all-gather | bytes 34816 | tf_op jit(solution)/shard_map/all_gather | solution.py:71
  344.8 0.0 all-to-all-done.2
  344.9 44.4 %while.11 = (s32[]{:T(128)}, f32[1024]{0:T(1024)S(1)}, pred[1024]{0:T(1024)(128)(4,1)S(1)}, bf16[8,2048]{1,0:T(8,128)(2,1)S(1)}, s32[8,2048]{1,0:T(8,128)S(1)}, ...) while((s32[]{:T(128)}, f32[1024]{0:T(1024)S(1)}, ...), condition=%wide.region_7.8_spmd.clone, body=%wide.region_5.7_spmd.clone.sunk | while | flops 3231719424 | bytes 4777595 | solution.py:30
  344.9 5.4 %fusion.21 = f32[1024]{0:T(1024)S(1)} fusion(bf16[1024,768]{1,0:T(8,128)(2,1)S(1)} %get-tuple-element.173, s32[1024]{0:T(1024)S(1)} %iota_add_fusion.2, s32[2048]{0:T(1024)S(1)} %bitcast.35, pred[1024]{0:T(1024)(128)(4,1)S(1)} %get-tuple-element.169, pred[2048]{0:T(1024)(128)(4,1)S(1)} %compare_reduce_fusion.2, ...), kind=kOutput, calls=%fused_computation.3.clone.1 | convolution fusion | flops 3231710208 | bytes 4738560 | tf_op jit(solution)/shard_map/while/body/eval_jaxpr/dot_general | solution.py:20
  350.5 5.4 %fusion.21 = f32[1024]{0:T(1024)S(1)} fusion(bf16[1024,768]{1,0:T(8,128)(2,1)S(1)} %get-tuple-element.173, s32[1024]{0:T(1024)S(1)} %iota_add_fusion.2, s32[2048]{0:T(1024)S(1)} %bitcast.35, pred[1024]{0:T(1024)(128)(4,1)S(1)} %get-tuple-element.169, pred[2048]{0:T(1024)(128)(4,1)S(1)} %compare_reduce_fusion.2, ...), kind=kOutput, calls=%fused_computation.3.clone.1 | convolution fusion | flops 3231710208 | bytes 4738560 | tf_op jit(solution)/shard_map/while/body/eval_jaxpr/dot_general | solution.py:20
  356.1 5.4 %fusion.21 = f32[1024]{0:T(1024)S(1)} fusion(bf16[1024,768]{1,0:T(8,128)(2,1)S(1)} %get-tuple-element.173, s32[1024]{0:T(1024)S(1)} %iota_add_fusion.2, s32[2048]{0:T(1024)S(1)} %bitcast.35, pred[1024]{0:T(1024)(128)(4,1)S(1)} %get-tuple-element.169, pred[2048]{0:T(1024)(128)(4,1)S(1)} %compare_reduce_fusion.2, ...), kind=kOutput, calls=%fused_computation.3.clone.1 | convolution fusion | flops 3231710208 | bytes 4738560 | tf_op jit(solution)/shard_map/while/body/eval_jaxpr/dot_general | solution.py:20
  361.6 5.4 %fusion.21 = f32[1024]{0:T(1024)S(1)} fusion(bf16[1024,768]{1,0:T(8,128)(2,1)S(1)} %get-tuple-element.173, s32[1024]{0:T(1024)S(1)} %iota_add_fusion.2, s32[2048]{0:T(1024)S(1)} %bitcast.35, pred[1024]{0:T(1024)(128)(4,1)S(1)} %get-tuple-element.169, pred[2048]{0:T(1024)(128)(4,1)S(1)} %compare_reduce_fusion.2, ...), kind=kOutput, calls=%fused_computation.3.clone.1 | convolution fusion | flops 3231710208 | bytes 4738560 | tf_op jit(solution)/shard_map/while/body/eval_jaxpr/dot_general | solution.py:20
  367.2 5.4 %fusion.21 = f32[1024]{0:T(1024)S(1)} fusion(bf16[1024,768]{1,0:T(8,128)(2,1)S(1)} %get-tuple-element.173, s32[1024]{0:T(1024)S(1)} %iota_add_fusion.2, s32[2048]{0:T(1024)S(1)} %bitcast.35, pred[1024]{0:T(1024)(128)(4,1)S(1)} %get-tuple-element.169, pred[2048]{0:T(1024)(128)(4,1)S(1)} %compare_reduce_fusion.2, ...), kind=kOutput, calls=%fused_computation.3.clone.1 | convolution fusion | flops 3231710208 | bytes 4738560 | tf_op jit(solution)/shard_map/while/body/eval_jaxpr/dot_general | solution.py:20
  372.7 5.4 %fusion.21 = f32[1024]{0:T(1024)S(1)} fusion(bf16[1024,768]{1,0:T(8,128)(2,1)S(1)} %get-tuple-element.173, s32[1024]{0:T(1024)S(1)} %iota_add_fusion.2, s32[2048]{0:T(1024)S(1)} %bitcast.35, pred[1024]{0:T(1024)(128)(4,1)S(1)} %get-tuple-element.169, pred[2048]{0:T(1024)(128)(4,1)S(1)} %compare_reduce_fusion.2, ...), kind=kOutput, calls=%fused_computation.3.clone.1 | convolution fusion | flops 3231710208 | bytes 4738560 | tf_op jit(solution)/shard_map/while/body/eval_jaxpr/dot_general | solution.py:20
  378.3 5.4 %fusion.21 = f32[1024]{0:T(1024)S(1)} fusion(bf16[1024,768]{1,0:T(8,128)(2,1)S(1)} %get-tuple-element.173, s32[1024]{0:T(1024)S(1)} %iota_add_fusion.2, s32[2048]{0:T(1024)S(1)} %bitcast.35, pred[1024]{0:T(1024)(128)(4,1)S(1)} %get-tuple-element.169, pred[2048]{0:T(1024)(128)(4,1)S(1)} %compare_reduce_fusion.2, ...), kind=kOutput, calls=%fused_computation.3.clone.1 | convolution fusion | flops 3231710208 | bytes 4738560 | tf_op jit(solution)/shard_map/while/body/eval_jaxpr/dot_general | solution.py:20
  383.8 5.4 %fusion.21 = f32[1024]{0:T(1024)S(1)} fusion(bf16[1024,768]{1,0:T(8,128)(2,1)S(1)} %get-tuple-element.173, s32[1024]{0:T(1024)S(1)} %iota_add_fusion.2, s32[2048]{0:T(1024)S(1)} %bitcast.35, pred[1024]{0:T(1024)(128)(4,1)S(1)} %get-tuple-element.169, pred[2048]{0:T(1024)(128)(4,1)S(1)} %compare_reduce_fusion.2, ...), kind=kOutput, calls=%fused_computation.3.clone.1 | convolution fusion | flops 3231710208 | bytes 4738560 | tf_op jit(solution)/shard_map/while/body/eval_jaxpr/dot_general | solution.py:20
  389.3 0.6 broadcast_maximum_fusion
  389.9 3.3 all-to-all-start.3
  393.3 7.6 %all-to-all-done.3 = f32[8,1,128]{2,1,0:T(1,128)S(1)} async-done(((f32[8,1,128]{2,1,0:T(1,128)}), f32[8,1,128]{2,1,0:T(1,128)S(1)}, u32[]{:S(2)}, u32[]{:S(2)}) %all-to-all-start.3) | async-done | bytes 4128 | tf_op jit(solution)/shard_map/all_to_all | solution.py:77
  400.9 3.4 gather_fusion
  (41 shorter events, 0.7 us)
Async XLA Ops:
  3.6 14.7 %all-to-all-start = ((bf16[8,1,128]{2,1,0:T(2,128)(2,1)}), bf16[8,1,128]{2,1,0:T(2,128)(2,1)S(1)}, u32[]{:S(2)}, u32[]{:S(2)}) async-start(bf16[8,1,128]{2,1,0:T(2,128)(2,1)} %compare_convert_fusion), calls=%async_computation | async-start | bytes 8192 | tf_op jit(solution)/shard_map/all_to_all | solution.py:62
  52.9 292.0 %all-to-all-start.2 = ((bf16[16,1024,768]{2,1,0:T(8,128)(2,1)}), bf16[16,1024,768]{2,1,0:T(8,128)(2,1)}, u32[]{:S(2)}, u32[]{:S(2)}) async-start(bf16[16,1024,768]{2,1,0:T(8,128)(2,1)} %stack.3), calls=%async_computation.2 | async-start | bytes 50331648 | tf_op jit(solution)/shard_map/all_to_all | solution.py:69
  389.9 11.0 %all-to-all-start.3 = ((f32[8,1,128]{2,1,0:T(1,128)}), f32[8,1,128]{2,1,0:T(1,128)S(1)}, u32[]{:S(2)}, u32[]{:S(2)}) async-start(f32[8,1,128]{2,1,0:T(1,128)} %bitcast.6), calls=%async_computation.3 | async-start | bytes 8192 | tf_op jit(solution)/shard_map/all_to_all | solution.py:77
